TPU v7x, 32 devices: a whole 2x2x4 slice. The times are simulated.
32 devices in a mesh: snp: 4 (over z), tile: 8 (over y, x, core).
Axes of the slice: x: 2, y: 2, z: 4, core: 2. Of those that a mesh axis runs over, the one named last changes fastest.
Arguments:
- dosages: float32 [16384, 8192], P('tile', 'snp'), may hold values from 0 to 2
- phenotypes: float32 [16384, 512], P('tile', 'snp'), may hold values from -6 to 6
Outputs:
- factor: float32 [16384, 512], P('tile')
- whitened: float32 [16384, 512], P('tile', 'snp')
All inputs are finite; a program needn't handle non-finite values.
Results may differ from a plain program's by a relative error of at most 0.00011.
Values sent between devices are 32-bit elements; how exact they have to be, the bound alone decides.
A program may use at most 128 MiB of HBM per device.

v0:
```python
import functools

import jax
import jax.numpy as jnp
from jax import lax
from jax.experimental import pallas as pl
from jax.experimental.pallas import tpu as pltpu
from jax.sharding import PartitionSpec as P

BLK = 256
HALF = BLK // 2
PIECES = 16
CHUNK = 64
MROWS = 256
SLAB = 64
MESH = pl.DeviceIdType.MESH
NT = (((1,), (1,)), ((), ()))


def split(value):
    high = value.astype(jnp.bfloat16)
    return high, (value - high.astype(jnp.float32)).astype(jnp.bfloat16)


def eliminate(work, first, last):
    below = lax.broadcasted_iota(jnp.int32, (SLAB, 1), 0)
    for j in range(first, last):
        column = jnp.where(below > j, work[:, j:j + 1], 0.0)
        work = work - column * (work[j:j + 1] * (1.0 / work[j:j + 1, j:j + 1]))
    return work


def slab_update(b, work, inverse, upper):
    wide = inverse.shape[0]
    exact = functools.partial(jnp.dot, precision=lax.Precision.HIGHEST, preferred_element_type=jnp.float32)
    r = lax.broadcasted_iota(jnp.int32, work.shape, 0)
    c = lax.broadcasted_iota(jnp.int32, work.shape, 1)
    pivots = jnp.sum(jnp.where(r == c, work, 0.0), axis=1, keepdims=True)
    work = work * lax.rsqrt(pivots)
    own = pl.ds(pl.multiple_of(b * SLAB, SLAB), SLAB)
    lane = lax.broadcasted_iota(jnp.int32, (SLAB, wide), 1)
    mine = (lane >= b * SLAB) & (lane < (b + 1) * SLAB)
    after = lane >= (b + 1) * SLAB
    upper_block = jnp.where(c < SLAB, jnp.where(c >= r, work, 0.0), 0.0)[:, :SLAB]
    inverse_block = work[:, SLAB:]
    repeat = wide // SLAB
    solved = exact(inverse_block, inverse[own])
    solved = jnp.where(mine, jnp.concatenate([inverse_block] * repeat, 1), solved)
    later = jnp.where(after, solved, 0.0)
    upper[own] = jnp.where(mine, jnp.concatenate([upper_block] * repeat, 1), later)
    inverse[own] = solved
    row_all = lax.broadcasted_iota(jnp.int32, (wide, wide), 0)
    lane_all = lax.broadcasted_iota(jnp.int32, (wide, wide), 1)
    cleared = (row_all >= (b + 1) * SLAB) & (lane_all >= b * SLAB) & (lane_all < (b + 1) * SLAB)
    inverse[...] = jnp.where(cleared, 0.0, inverse[...]) - exact(later.T, solved)


def kernel(n_tile, n_snp, dos_hbm, phe_hbm, cross_hbm, inverse_hbm, upper_hbm, heads_hbm,
           dos, panels, heads, diag, inverse, upper, work, high, low, counts, mean, scale, x, oin, iin,
           load_sem, head_sem, out_sem, cnt_send, cnt_recv,
           a_send, a_recv, b_send, b_recv, sa_send, sa_recv, sb_send, sb_recv,
           da_send, da_recv, db_send, db_recv, ea_send, ea_recv, eb_send, eb_recv,
           i_send, o_recv, o_send, i_recv):
    rows, snps = dos.shape
    wide = 2 * BLK
    tile = lax.axis_index("tile")
    snp = lax.axis_index("snp")
    chips = n_tile // 2
    across = chips // 2
    core = lax.rem(tile, 2)
    chip = lax.div(tile, 2)
    pos = jnp.where(chip < across, chip, chips + across - 1 - chip)
    sib = chip * 2 + 1 - core

    def at_pos(q):
        q = lax.rem(q + chips, chips)
        return 2 * jnp.where(q < across, q, chips + across - 1 - q) + core

    right, left = at_pos(pos + 1), at_pos(pos - 1)
    half = n_snp // 2
    lower = snp < half
    depth = jnp.where(lower, snp, n_snp - 1 - snp)
    inner = jnp.where(lower, snp + 1, snp - 1)
    outer = jnp.where(lower, snp - 1, snp + 1)
    middle = depth == half - 1
    has_outer = depth > 0

    barrier = pltpu.get_barrier_semaphore()
    for d in range(1, n_tile):
        pl.semaphore_signal(barrier, inc=1, device_id={"tile": lax.rem(tile + d, n_tile)}, device_id_type=MESH)
    pl.semaphore_signal(barrier, inc=1, device_id={"snp": inner}, device_id_type=MESH)

    @pl.when(has_outer)
    def _():
        pl.semaphore_signal(barrier, inc=1, device_id={"snp": outer}, device_id_type=MESH)

    def load(k):
        r = pl.ds(pl.multiple_of(k * MROWS, MROWS), MROWS)
        return pltpu.make_async_copy(dos_hbm.at[r], dos.at[r], load_sem.at[k])

    n_load = rows // MROWS
    own = pl.ds(pl.multiple_of(core * BLK, BLK), BLK)
    own_panel = pltpu.make_async_copy(dos_hbm.at[pl.ds(0, BLK)], panels.at[own], head_sem.at[0])
    own_heads = pltpu.make_async_copy(phe_hbm.at[pl.ds(0, BLK)], heads.at[own], head_sem.at[1])

    @pl.when(pos == 0)
    def _():
        own_panel.start()
        own_heads.start()

    for k in range(n_load):
        load(k).start()
    pl.semaphore_wait(barrier, n_tile + jnp.where(has_outer, 1, 0))

    @pl.when(pos == 0)
    def _():
        own_panel.wait()
        own_heads.wait()

    def remote(ref, send, recv, **where):
        return pltpu.make_async_remote_copy(src_ref=ref, dst_ref=ref, send_sem=send, recv_sem=recv,
                                            device_id=where, device_id_type=MESH)

    def piece(buf, which, side, k, size):
        return buf.at[pl.ds(pl.multiple_of(which * BLK + side * HALF + k * size, size), size)]

    def ring_step(buf, size, sems, k_a, k_b, last, index_a, index_b):
        (asn, arc, bsn, brc, sas, sar, sbs, sbr) = sems

        @pl.when((k_a >= 0) & (k_a < last))
        def _():
            ref = piece(buf, core, 0, k_a, size)
            i = index_a
            d = remote(ref, asn.at[i], arc.at[i], tile=right)

            @pl.when(pos > 0)
            def _():
                d.wait_recv()

            @pl.when(pos < chips - 1)
            def _():
                d.start()

            remote(ref, sas.at[i], sar.at[i], tile=sib).start()

        @pl.when((k_b >= 0) & (k_b < last))
        def _():
            ref = piece(buf, core, 1, k_b, size)
            i = index_b
            d = remote(ref, bsn.at[i], brc.at[i], tile=left)

            @pl.when(pos > 0)
            def _():
                d.wait_recv()

            @pl.when(pos != 1)
            def _():
                d.start()

            remote(ref, sbs.at[i], sbr.at[i], tile=sib).start()

    def sibling_wait(buf, size, sems, k, i):
        (asn, arc, bsn, brc, sas, sar, sbs, sbr) = sems
        remote(piece(buf, 1 - core, 0, k, size), sas.at[i], sar.at[i], tile=sib).wait_recv()
        remote(piece(buf, 1 - core, 1, k, size), sbs.at[i], sbr.at[i], tile=sib).wait_recv()

    def drain(buf, size, sems, k, i):
        (asn, arc, bsn, brc, sas, sar, sbs, sbr) = sems
        ref_a, ref_b = piece(buf, core, 0, k, size), piece(buf, core, 1, k, size)

        @pl.when(pos < chips - 1)
        def _():
            remote(ref_a, asn.at[i], arc.at[i], tile=right).wait_send()

        @pl.when(pos != 1)
        def _():
            remote(ref_b, bsn.at[i], brc.at[i], tile=left).wait_send()

        remote(ref_a, sas.at[i], sar.at[i], tile=sib).wait_send()
        remote(ref_b, sbs.at[i], sbr.at[i], tile=sib).wait_send()

    ring = (a_send, a_recv, b_send, b_recv, sa_send, sa_recv, sb_send, sb_recv)
    dring = (da_send, da_recv, db_send, db_recv, ea_send, ea_recv, eb_send, eb_recv)
    psize = HALF // PIECES
    start_b = lax.rem(chips - pos, chips)

    def count_copy(d):
        ref = counts.at[tile]
        return remote(ref, cnt_send.at[d], cnt_recv.at[tile], tile=lax.rem(tile + d, n_tile))

    def ring_slot(s, total):
        @pl.when(s < n_load)
        def _():
            load(s).wait()
        r = jnp.minimum(s, n_load - 1)
        part = jnp.sum(dos[pl.ds(pl.multiple_of(r * MROWS, MROWS), MROWS)].reshape(MROWS // 8, 8, snps), axis=0)
        total = total + jnp.where(s < n_load, part, 0.0)
        ring_step(panels, psize, ring, s - pos, s - start_b, PIECES, s - pos, s - start_b)
        return total

    total = lax.fori_loop(0, n_load, ring_slot, jnp.zeros((8, snps), jnp.float32))
    counts[tile] = jnp.sum(total, axis=0, keepdims=True)
    for d in range(1, n_tile):
        count_copy(d).start()

    def ring_rest(s, carry):
        ring_step(panels, psize, ring, s - pos, s - start_b, PIECES, s - pos, s - start_b)
        return carry

    lax.fori_loop(n_load, PIECES + chips, ring_rest, 0)
    for d in range(1, n_tile):
        source = lax.rem(tile + d, n_tile)
        remote(counts.at[source], cnt_send.at[d], cnt_recv.at[source], tile=source).wait_recv()
    freq = counts[0]
    for t in range(1, n_tile):
        freq = freq + counts[t]
    freq = freq / (2.0 * rows * n_tile)
    mean[...] = 2.0 * freq
    scale[...] = lax.rsqrt(jnp.maximum(2.0 * freq * (1.0 - freq), 0.05))
    ring_step(heads, HALF, ring, 0, jnp.where(pos == 0, 0, -1), 1, PIECES, PIECES)

    @pl.when(pos > 0)
    def _():
        ring_step(heads, HALF, ring, -1, 0, 1, PIECES, PIECES)

    def wait_sib(k, carry):
        sibling_wait(panels, psize, ring, k, k)
        return carry

    lax.fori_loop(0, PIECES, wait_sib, 0)

    def standardize(k, carry):
        r = pl.ds(pl.multiple_of(k * 64, 64), 64)
        h, l = split((panels[r] - mean[...]) * scale[...])
        high[r] = h
        low[r] = l
        return carry

    lax.fori_loop(0, wide // 64, standardize, 0)

    n_chunk = rows // CHUNK
    per = MROWS // CHUNK
    inverse_count = 1.0 / (snps * n_snp)

    def rows_of(buf, k):
        return buf.at[pl.ds(pl.multiple_of(k * CHUNK, CHUNK), CHUNK)]

    def to_inner(k):
        return [
            pltpu.make_async_remote_copy(src_ref=rows_of(x, k), dst_ref=rows_of(dst, k), send_sem=i_send.at[k],
                                         recv_sem=recv.at[k], device_id={"snp": inner}, device_id_type=MESH)
            for dst, recv in ((oin, o_recv), (iin, i_recv))
        ]

    def to_outer(k):
        return remote(rows_of(iin, k), o_send.at[k], i_recv.at[k], snp=outer)

    def to_hbm(k):
        return pltpu.make_async_copy(rows_of(iin, k), rows_of(cross_hbm, k), out_sem.at[k])

    b_shift = half + (half - 1 - depth)
    heads_d = BLK // CHUNK
    dsize = HALF // heads_d

    def slot(s, carry):
        @pl.when((lax.rem(s, per) == 0) & (s < n_chunk))
        def _():
            r = pl.ds(pl.multiple_of(lax.div(s, per) * MROWS, MROWS), MROWS)
            h, l = split((dos[r] - mean[...]) * scale[...])
            dot = functools.partial(lax.dot_general, dimension_numbers=NT, preferred_element_type=jnp.float32)
            x[r] = (dot(h, high[...]) + (dot(h, low[...]) + dot(l, high[...]))) * inverse_count

        k_a = s - depth

        @pl.when((k_a >= 0) & (k_a < n_chunk))
        def _():
            plain, across_copy = to_inner(k_a)

            @pl.when(has_outer)
            def _():
                plain.wait_recv()
                r = pl.ds(pl.multiple_of(k_a * CHUNK, CHUNK), CHUNK)
                x[r] = x[r] + oin[r]

            @pl.when(middle)
            def _():
                across_copy.start()

            @pl.when(jnp.logical_not(middle))
            def _():
                plain.start()

        k_b = s - b_shift

        @pl.when((k_b >= 0) & (k_b < n_chunk))
        def _():
            to_outer(k_b).wait_recv()

            @pl.when(middle)
            def _():
                r = pl.ds(pl.multiple_of(k_b * CHUNK, CHUNK), CHUNK)
                iin[r] = x[r] + iin[r]

            @pl.when(has_outer)
            def _():
                to_outer(k_b).start()

            to_hbm(k_b).start()

            @pl.when((k_b < heads_d) & (pos == 0))
            def _():
                r = pl.ds(pl.multiple_of(k_b * CHUNK, CHUNK), CHUNK)
                diag[pl.ds(pl.multiple_of(core * BLK + k_b * CHUNK, CHUNK), CHUNK)] = iin[r]

        k_d = s - b_shift - heads_d
        ring_step(diag, dsize, dring, k_d - pos, k_d - start_b, heads_d, k_d - pos, k_d - start_b)

        @pl.when(k_d == heads_d + chips - 1)
        def _():
            for k in range(heads_d):
                sibling_wait(diag, dsize, dring, k, k)
            r = lax.broadcasted_iota(jnp.int32, (wide, wide), 0)
            c = lax.broadcasted_iota(jnp.int32, (wide, wide), 1)
            inverse[...] = diag[...] + jnp.where(r == c, 1.0, 0.0)

        k_c = k_d - (heads_d + chips)
        slab = lax.div(k_c, 2)

        @pl.when((k_c >= 0) & (slab < wide // SLAB) & (lax.rem(k_c, 2) == 0))
        def _():
            own = pl.ds(pl.multiple_of(slab * SLAB, SLAB), SLAB)
            pair = pl.ds(pl.multiple_of(lax.div(slab, 2) * 2 * SLAB, 2 * SLAB), 2 * SLAB)
            block = inverse[own, pair]
            block = jnp.where(lax.rem(slab, 2) == 0, block[:, :SLAB], block[:, SLAB:])
            r = lax.broadcasted_iota(jnp.int32, (SLAB, SLAB), 0)
            c = lax.broadcasted_iota(jnp.int32, (SLAB, SLAB), 1)
            start = jnp.concatenate([block, jnp.where(r == c, 1.0, 0.0)], 1)
            work[...] = eliminate(start, 0, SLAB // 2)

        @pl.when((k_c >= 0) & (slab < wide // SLAB) & (lax.rem(k_c, 2) == 1))
        def _():
            slab_update(slab, eliminate(work[...], SLAB // 2, SLAB), inverse, upper)

        return carry

    lax.fori_loop(0, n_chunk + 2 * half, slot, 0)
    sibling_wait(heads, HALF, ring, 0, PIECES)
    r = lax.broadcasted_iota(jnp.int32, (wide, wide), 0)
    c = lax.broadcasted_iota(jnp.int32, (wide, wide), 1)
    inverse[...] = jnp.where(r >= c, inverse[...], 0.0)
    out_d = pltpu.make_async_copy(inverse, inverse_hbm, head_sem.at[0])
    out_u = pltpu.make_async_copy(upper, upper_hbm, head_sem.at[2])
    out_u.start()
    out_h = pltpu.make_async_copy(heads, heads_hbm, head_sem.at[1])
    out_d.start()
    out_h.start()

    def finish(k, carry):
        to_inner(k)[0].wait_send()

        @pl.when(has_outer)
        def _():
            to_outer(k).wait_send()

        to_hbm(k).wait()
        return carry

    lax.fori_loop(0, n_chunk, finish, 0)

    def drain_ring(k, carry):
        drain(panels, psize, ring, k, k)
        return carry

    lax.fori_loop(0, PIECES, drain_ring, 0)
    drain(heads, HALF, ring, 0, PIECES)
    for k in range(heads_d):
        drain(diag, dsize, dring, k, k)
    for d in range(1, n_tile):
        count_copy(d).wait_send()
    out_d.wait()
    out_u.wait()
    out_h.wait()


def gather_cross(dosages, phenotypes, n_tile, n_snp):
    rows, snps = dosages.shape
    wide = 2 * BLK
    f32 = jnp.float32
    n_chunk = rows // CHUNK
    dma = pltpu.SemaphoreType.DMA
    return pl.pallas_call(
        functools.partial(kernel, n_tile, n_snp),
        out_shape=(
            jax.ShapeDtypeStruct((rows, wide), f32),
            jax.ShapeDtypeStruct((wide, wide), f32),
            jax.ShapeDtypeStruct((wide, wide), f32),
            jax.ShapeDtypeStruct((wide, phenotypes.shape[1]), f32),
        ),
        in_specs=[pl.BlockSpec(memory_space=pl.ANY)] * 2,
        out_specs=[pl.BlockSpec(memory_space=pl.ANY)] * 4,
        scratch_shapes=[
            pltpu.VMEM((rows, snps), f32),
            pltpu.VMEM((wide, snps), f32),
            pltpu.VMEM((wide, phenotypes.shape[1]), f32),
            pltpu.VMEM((wide, wide), f32),
            pltpu.VMEM((wide, wide), f32),
            pltpu.VMEM((wide, wide), f32),
            pltpu.VMEM((SLAB, 2 * SLAB), f32),
            pltpu.VMEM((wide, snps), jnp.bfloat16),
            pltpu.VMEM((wide, snps), jnp.bfloat16),
            pltpu.VMEM((n_tile, 1, snps), f32),
            pltpu.VMEM((1, snps), f32),
            pltpu.VMEM((1, snps), f32),
            pltpu.VMEM((rows, wide), f32),
            pltpu.VMEM((rows, wide), f32),
            pltpu.VMEM((rows, wide), f32),
            dma((rows // MROWS,)),
            dma((3,)),
            dma((n_chunk,)),
            dma((n_tile,)),
            dma((n_tile,)),
        ]
        + [dma((PIECES + 1,))] * 8
        + [dma((BLK // CHUNK,))] * 8
        + [dma((n_chunk,))] * 4,
        compiler_params=pltpu.CompilerParams(
            collective_id=0, has_side_effects=True, vmem_limit_bytes=58 * 1024 * 1024
        ),
    )(dosages, phenotypes)


def body(dosages, phenotypes):
    n_tile = lax.axis_size("tile")
    n_snp = lax.axis_size("snp")
    tile_index = lax.axis_index("tile")
    cross, inverse, upper, heads = gather_cross(dosages, phenotypes, n_tile, n_snp)
    exact = functools.partial(lax.dot_general, precision=lax.Precision.HIGHEST, preferred_element_type=jnp.float32)
    factor = exact(cross, inverse, NT)
    lower = upper.T
    solved = jnp.dot(inverse, heads, precision=lax.Precision.HIGHEST)
    head_rows = jnp.where(
        tile_index == 0, lower[:BLK], jnp.where(tile_index == 1, lower[BLK:], factor[:BLK])
    )
    factor = factor.at[:BLK].set(head_rows)
    current = phenotypes - jnp.dot(factor, solved, precision=lax.Precision.HIGHEST)
    head = jnp.where(tile_index == 0, solved[:BLK], jnp.where(tile_index == 1, solved[BLK:], current[:BLK]))
    return (factor, current.at[:BLK].set(head))


def solution(mesh):
    placed = (P("tile", "snp"), P("tile", "snp"))
    return jax.shard_map(
        body,
        mesh=mesh,
        in_specs=placed,
        out_specs=(P("tile", None), P("tile", "snp")),
        check_vma=False,
    )
```

profile of v0, /device:TPU:2, one launch (start us, length us, event | category | flops | bytes accessed | tf_op | source)
XLA Modules:
  0.0 247.8 jit_solution(17211185385660565278)
XLA Ops:
  0.6 226.4 %shard_map.41 = (f32[2048,512]{1,0:T(8,128)}, f32[512,512]{1,0:T(8,128)}, f32[512,512]{1,0:T(8,128)}, f32[512,128]{1,0:T(8,128)}) custom-call(f32[2048,2048]{1,0:T(8,128)} %dos_hbm.1, f32[2048,128]{1,0:T(8,128)} %phe_hbm.1), custom_call_target="tpu_custom_call" | custom-call | tf_op jit(solution)/shard_map/pallas_call | solution.py:391
  227.0 8.8 %fusion.3 = f32[2048,512]{1,0:T(8,128)S(1)} fusion(f32[2048,512]{1,0:T(8,128)} %get-tuple-element.30, f32[512,512]{1,0:T(8,128)} %get-tuple-element.31), kind=kOutput, calls=%fused_computation.7 | convolution fusion | flops 6442450944 | bytes 9437184 | tf_op jit(solution)/shard_map/dot_general | solution.py:438
  235.8 0.0 copy-start
  235.8 2.0 copy-done
  237.8 0.0 copy-start.2
  237.9 0.0 copy-start.4
  237.9 0.0 copy-start.1
  237.9 0.2 copy.6
  238.1 1.4 fusion
  239.5 0.2 copy.5
  239.7 0.8 constant_dynamic-update-slice_fusion
  240.6 0.0 copy-done.2
  240.6 0.0 copy-done.4
  240.6 1.0 fusion.4
  241.6 0.0 copy-done.1
  241.6 5.2 %convolution_subtract_fusion = f32[2048,128]{1,0:T(8,128)S(1)} fusion(f32[2048,128]{1,0:T(8,128)S(1)} %copy-done.1, f32[2048,512]{1,0:T(8,128)} %constant_dynamic-update-slice_fusion, f32[512,128]{1,0:T(8,128)S(1)} %fusion.4), kind=kOutput, calls=%fused_computation | convolution fusion | flops 1610874880 | bytes 6553600 | tf_op jit(solution)/shard_map/dot_general | solution.py:445
  246.8 0.1 fusion.2
  246.9 0.0 copy-start.3
  246.9 1.0 copy-done.3
  (1 shorter events, 0.0 us)
Async XLA Ops:
  235.8 2.0 copy-start
  237.8 2.7 %copy-start.2 = (f32[512,512]{1,0:T(8,128)S(1)}, f32[512,512]{1,0:T(8,128)}, u32[]{:S(2)}) copy-start(f32[512,512]{1,0:T(8,128)} %get-tuple-element.31) | copy-start | bytes 3145732
  237.9 2.7 %copy-start.4 = (f32[512,128]{1,0:T(8,128)S(1)}, f32[512,128]{1,0:T(8,128)}, u32[]{:S(2)}) copy-start(f32[512,128]{1,0:T(8,128)} %get-tuple-element.33) | copy-start | bytes 786436
  237.9 3.7 %copy-start.1 = (f32[2048,128]{1,0:T(8,128)S(1)}, f32[2048,128]{1,0:T(8,128)}, u32[]{:S(2)}) copy-start(f32[2048,128]{1,0:T(8,128)} %phe_hbm.1) | copy-start | bytes 3145732
  246.9 1.0 copy-start.3
where the time goes:
time: 248 us
  Pallas kernels  226 us (91%)
  matrix products  15 us (6%)
  local copies, waits for them, and re-layouts  4.24 us (2%)
    pallas_call x1, Pallas kernels, gather_cross(): pl.pallas_call(functools.partial(kernel, n_tile, n_snp), out_shape=(jax.S...  226 us
    dot_general x1, matrix products, body(): factor = exact(cross, inverse, NT)  8.81 us
    dot_general x1, matrix products, body(): jnp.dot(factor, solved, precision=lax.Precision.HIGHEST)  5.21 us

commit v1 on v0

--- a/solution.py
+++ b/solution.py
@@ -10,7 +10,9 @@
 BLK = 256
 HALF = BLK // 2
 PIECES = 16
-CHUNK = 64
+GROUPS = 4
+HOP = 2
+DIAG_PIECES = 4
 MROWS = 256
 SLAB = 64
 MESH = pl.DeviceIdType.MESH
@@ -122,7 +124,7 @@
                                             device_id=where, device_id_type=MESH)
 
     def piece(buf, which, side, k, size):
-        return buf.at[pl.ds(pl.multiple_of(which * BLK + side * HALF + k * size, size), size)]
+        return buf.at[pl.ds(pl.multiple_of(which * BLK + (2 * k + side) * size, size), size)]
 
     def ring_step(buf, size, sems, k_a, k_b, last, index_a, index_b):
         (asn, arc, bsn, brc, sas, sar, sbs, sbr) = sems
@@ -198,6 +200,7 @@
         ring_step(panels, psize, ring, s - pos, s - start_b, PIECES, s - pos, s - start_b)
         return total
 
+    first = max(n_load, PIECES // GROUPS + chips)
     total = lax.fori_loop(0, n_load, ring_slot, jnp.zeros((8, snps), jnp.float32))
     counts[tile] = jnp.sum(total, axis=0, keepdims=True)
     for d in range(1, n_tile):
@@ -207,7 +210,7 @@
         ring_step(panels, psize, ring, s - pos, s - start_b, PIECES, s - pos, s - start_b)
         return carry
 
-    lax.fori_loop(n_load, PIECES + chips, ring_rest, 0)
+    lax.fori_loop(n_load, first, ring_rest, 0)
     for d in range(1, n_tile):
         source = lax.rem(tile + d, n_tile)
         remote(counts.at[source], cnt_send.at[d], cnt_recv.at[source], tile=source).wait_recv()
@@ -217,33 +220,39 @@
     freq = freq / (2.0 * rows * n_tile)
     mean[...] = 2.0 * freq
     scale[...] = lax.rsqrt(jnp.maximum(2.0 * freq * (1.0 - freq), 0.05))
-    ring_step(heads, HALF, ring, 0, jnp.where(pos == 0, 0, -1), 1, PIECES, PIECES)
-
-    @pl.when(pos > 0)
-    def _():
-        ring_step(heads, HALF, ring, -1, 0, 1, PIECES, PIECES)
 
     def wait_sib(k, carry):
         sibling_wait(panels, psize, ring, k, k)
         return carry
 
-    lax.fori_loop(0, PIECES, wait_sib, 0)
-
-    def standardize(k, carry):
-        r = pl.ds(pl.multiple_of(k * 64, 64), 64)
-        h, l = split((panels[r] - mean[...]) * scale[...])
-        high[r] = h
-        low[r] = l
-        return carry
-
-    lax.fori_loop(0, wide // 64, standardize, 0)
-
-    n_chunk = rows // CHUNK
-    per = MROWS // CHUNK
+    gsize = BLK // GROUPS
+
+    def standardize(g, carry):
+        for p in range(2):
+            source = pl.ds(pl.multiple_of(p * BLK + g * gsize, gsize), gsize)
+            target = pl.ds(pl.multiple_of((2 * g + p) * gsize, gsize), gsize)
+            h, l = split((panels[source] - mean[...]) * scale[...])
+            high[target] = h
+            low[target] = l
+        return carry
+
+    lax.fori_loop(0, PIECES // GROUPS, wait_sib, 0)
+    standardize(0, 0)
+
+    per = rows // MROWS
+    n_chunk = per * GROUPS
+    lanes = wide // GROUPS
     inverse_count = 1.0 / (snps * n_snp)
 
     def rows_of(buf, k):
-        return buf.at[pl.ds(pl.multiple_of(k * CHUNK, CHUNK), CHUNK)]
+        return buf.at[pl.ds(pl.multiple_of(k * MROWS, MROWS), MROWS)]
+
+    def place(k):
+        late = jnp.maximum(k - (per + GROUPS - 1), 0)
+        early = k < per + GROUPS - 1
+        group = jnp.where(k < per, 0, jnp.where(early, k - per + 1, 1 + lax.div(late, per - 1)))
+        block = jnp.where(k < per, k, jnp.where(early, 0, 1 + lax.rem(late, per - 1)))
+        return group, block
 
     def to_inner(k):
         return [
@@ -256,21 +265,43 @@
         return remote(rows_of(iin, k), o_send.at[k], i_recv.at[k], snp=outer)
 
     def to_hbm(k):
-        return pltpu.make_async_copy(rows_of(iin, k), rows_of(cross_hbm, k), out_sem.at[k])
-
-    b_shift = half + (half - 1 - depth)
-    heads_d = BLK // CHUNK
+        group, block = place(k)
+        r = pl.ds(pl.multiple_of(block * MROWS, MROWS), MROWS)
+        c = pl.ds(pl.multiple_of(group * lanes, lanes), lanes)
+        return pltpu.make_async_copy(rows_of(iin, k), cross_hbm.at[r, c], out_sem.at[k])
+
+    b_shift = HOP * (half + (half - 1 - depth))
+    heads_d = DIAG_PIECES
     dsize = HALF // heads_d
+    ready = per + GROUPS - 2
 
     def slot(s, carry):
-        @pl.when((lax.rem(s, per) == 0) & (s < n_chunk))
-        def _():
-            r = pl.ds(pl.multiple_of(lax.div(s, per) * MROWS, MROWS), MROWS)
+        for i in range(2):
+            k_r = first + 2 * s + i
+            ring_step(panels, psize, ring, k_r - pos, k_r - start_b, PIECES, k_r - pos, k_r - start_b)
+
+        @pl.when(s == per - 1)
+        def _():
+            ring_step(heads, HALF, ring, 0, jnp.where(pos == 0, 0, -1), 1, PIECES, PIECES)
+
+            @pl.when(pos > 0)
+            def _():
+                ring_step(heads, HALF, ring, -1, 0, 1, PIECES, PIECES)
+
+            lax.fori_loop(PIECES // GROUPS, PIECES, wait_sib, 0)
+            lax.fori_loop(1, GROUPS, standardize, 0)
+
+        @pl.when(s < n_chunk)
+        def _():
+            group, block = place(s)
+            r = pl.ds(pl.multiple_of(block * MROWS, MROWS), MROWS)
+            g = pl.ds(pl.multiple_of(group * lanes, lanes), lanes)
             h, l = split((dos[r] - mean[...]) * scale[...])
             dot = functools.partial(lax.dot_general, dimension_numbers=NT, preferred_element_type=jnp.float32)
-            x[r] = (dot(h, high[...]) + (dot(h, low[...]) + dot(l, high[...]))) * inverse_count
-
-        k_a = s - depth
+            value = dot(h, high[g]) + (dot(h, low[g]) + dot(l, high[g]))
+            x[pl.ds(pl.multiple_of(s * MROWS, MROWS), MROWS)] = value * inverse_count
+
+        k_a = s - HOP * depth
 
         @pl.when((k_a >= 0) & (k_a < n_chunk))
         def _():
@@ -279,7 +310,7 @@
             @pl.when(has_outer)
             def _():
                 plain.wait_recv()
-                r = pl.ds(pl.multiple_of(k_a * CHUNK, CHUNK), CHUNK)
+                r = pl.ds(pl.multiple_of(k_a * MROWS, MROWS), MROWS)
                 x[r] = x[r] + oin[r]
 
             @pl.when(middle)
@@ -298,7 +329,7 @@
 
             @pl.when(middle)
             def _():
-                r = pl.ds(pl.multiple_of(k_b * CHUNK, CHUNK), CHUNK)
+                r = pl.ds(pl.multiple_of(k_b * MROWS, MROWS), MROWS)
                 iin[r] = x[r] + iin[r]
 
             @pl.when(has_outer)
@@ -307,30 +338,32 @@
 
             to_hbm(k_b).start()
 
-            @pl.when((k_b < heads_d) & (pos == 0))
-            def _():
-                r = pl.ds(pl.multiple_of(k_b * CHUNK, CHUNK), CHUNK)
-                diag[pl.ds(pl.multiple_of(core * BLK + k_b * CHUNK, CHUNK), CHUNK)] = iin[r]
-
-        k_d = s - b_shift - heads_d
-        ring_step(diag, dsize, dring, k_d - pos, k_d - start_b, heads_d, k_d - pos, k_d - start_b)
-
-        @pl.when(k_d == heads_d + chips - 1)
-        def _():
+        @pl.when(k_b == ready)
+        def _():
+            @pl.when(pos == 0)
+            def _():
+                parts = [iin[k * MROWS:(k + 1) * MROWS] for k in (0, *range(per, per + GROUPS - 1))]
+                diag[own] = jnp.concatenate([p[:, :gsize] for p in parts] + [p[:, gsize:] for p in parts], 1)
+
+            def diag_slot(k_d, carry):
+                ring_step(diag, dsize, dring, k_d - pos, k_d - start_b, heads_d, k_d - pos, k_d - start_b)
+                return carry
+
+            lax.fori_loop(0, heads_d + chips - 1, diag_slot, 0)
             for k in range(heads_d):
                 sibling_wait(diag, dsize, dring, k, k)
             r = lax.broadcasted_iota(jnp.int32, (wide, wide), 0)
             c = lax.broadcasted_iota(jnp.int32, (wide, wide), 1)
             inverse[...] = diag[...] + jnp.where(r == c, 1.0, 0.0)
 
-        k_c = k_d - (heads_d + chips)
+        k_c = k_b - ready - 1
         slab = lax.div(k_c, 2)
 
         @pl.when((k_c >= 0) & (slab < wide // SLAB) & (lax.rem(k_c, 2) == 0))
         def _():
-            own = pl.ds(pl.multiple_of(slab * SLAB, SLAB), SLAB)
+            mine = pl.ds(pl.multiple_of(slab * SLAB, SLAB), SLAB)
             pair = pl.ds(pl.multiple_of(lax.div(slab, 2) * 2 * SLAB, 2 * SLAB), 2 * SLAB)
-            block = inverse[own, pair]
+            block = inverse[mine, pair]
             block = jnp.where(lax.rem(slab, 2) == 0, block[:, :SLAB], block[:, SLAB:])
             r = lax.broadcasted_iota(jnp.int32, (SLAB, SLAB), 0)
             c = lax.broadcasted_iota(jnp.int32, (SLAB, SLAB), 1)
@@ -343,7 +376,7 @@
 
         return carry
 
-    lax.fori_loop(0, n_chunk + 2 * half, slot, 0)
+    lax.fori_loop(0, n_chunk + HOP * (n_snp - 1) + 1, slot, 0)
     sibling_wait(heads, HALF, ring, 0, PIECES)
     r = lax.broadcasted_iota(jnp.int32, (wide, wide), 0)
     c = lax.broadcasted_iota(jnp.int32, (wide, wide), 1)
@@ -386,7 +419,8 @@
     rows, snps = dosages.shape
     wide = 2 * BLK
     f32 = jnp.float32
-    n_chunk = rows // CHUNK
+    n_chunk = rows // MROWS * GROUPS
+    lanes = wide // GROUPS
     dma = pltpu.SemaphoreType.DMA
     return pl.pallas_call(
         functools.partial(kernel, n_tile, n_snp),
@@ -411,9 +445,9 @@
             pltpu.VMEM((n_tile, 1, snps), f32),
             pltpu.VMEM((1, snps), f32),
             pltpu.VMEM((1, snps), f32),
-            pltpu.VMEM((rows, wide), f32),
-            pltpu.VMEM((rows, wide), f32),
-            pltpu.VMEM((rows, wide), f32),
+            pltpu.VMEM((rows * GROUPS, lanes), f32),
+            pltpu.VMEM((rows * GROUPS, lanes), f32),
+            pltpu.VMEM((rows * GROUPS, lanes), f32),
             dma((rows // MROWS,)),
             dma((3,)),
             dma((n_chunk,)),
@@ -421,7 +455,7 @@
             dma((n_tile,)),
         ]
         + [dma((PIECES + 1,))] * 8
-        + [dma((BLK // CHUNK,))] * 8
+        + [dma((DIAG_PIECES,))] * 8
         + [dma((n_chunk,))] * 4,
         compiler_params=pltpu.CompilerParams(
             collective_id=0, has_side_effects=True, vmem_limit_bytes=58 * 1024 * 1024
@@ -435,7 +469,9 @@
     tile_index = lax.axis_index("tile")
     cross, inverse, upper, heads = gather_cross(dosages, phenotypes, n_tile, n_snp)
     exact = functools.partial(lax.dot_general, precision=lax.Precision.HIGHEST, preferred_element_type=jnp.float32)
-    factor = exact(cross, inverse, NT)
+    wide = 2 * BLK
+    ordered = inverse.reshape(wide, 2, GROUPS, BLK // GROUPS).transpose(0, 2, 1, 3).reshape(wide, wide)
+    factor = exact(cross, ordered, NT)
     lower = upper.T
     solved = jnp.dot(inverse, heads, precision=lax.Precision.HIGHEST)
     head_rows = jnp.where(

time: 248 us -> 232 us (0.935)
  Pallas kernels: 226 us -> 207 us
    pallas_call x1, Pallas kernels: 226 us -> 207 us  [gather_cross(): pl.pallas_call(functools.partial(kernel, n_tile, n_snp), out_shape=(jax.S...]
where the time goes in v1:
time: 232 us; the launch traced here: 231 us
  Pallas kernels  207 us (89%)
  matrix products  16 us (7%)
  local copies, waits for them, and re-layouts  5.86 us (3%)
    pallas_call x1, Pallas kernels, gather_cross(): pl.pallas_call(functools.partial(kernel, n_tile, n_snp), out_shape=(jax.S...  207 us
    dot_general x1, matrix products, body(): factor = exact(cross, ordered, NT)  8.51 us
    dot_general x1, matrix products, body(): jnp.dot(factor, solved, precision=lax.Precision.HIGHEST)  5.23 us

profile of v1, /device:TPU:2, one launch (start us, length us, event | category | flops | bytes accessed | tf_op | source)
XLA Modules:
  0.0 231.3 jit_solution(8025729748251633823)
XLA Ops:
  0.6 207.3 %shard_map.41 = (f32[2048,512]{1,0:T(8,128)}, f32[512,512]{1,0:T(8,128)}, f32[512,512]{1,0:T(8,128)}, f32[512,128]{1,0:T(8,128)}) custom-call(f32[2048,2048]{1,0:T(8,128)} %dos_hbm.1, f32[2048,128]{1,0:T(8,128)} %phe_hbm.1), custom_call_target="tpu_custom_call" | custom-call | tf_op jit(solution)/shard_map/pallas_call | solution.py:425
  208.0 2.2 fusion.4
  210.2 1.6 copy.6
  211.8 0.1 copy.7
  211.9 8.5 %fusion.3 = f32[2048,512]{1,0:T(8,128)S(1)} fusion(f32[2048,512]{1,0:T(8,128)} %get-tuple-element.30, f32[512,512]{0,1:T(8,128)S(1)} %bitcast.12), kind=kOutput, calls=%fused_computation.7 | convolution fusion | flops 6442450944 | bytes 9437184 | tf_op jit(solution)/shard_map/dot_general | solution.py:474
  220.4 0.0 copy-start
  220.4 2.0 copy-done
  222.4 0.0 copy-start.1
  222.5 0.2 copy.10
  222.7 1.4 fusion
  224.0 0.2 copy.9
  224.2 0.8 constant_dynamic-update-slice_fusion
  225.1 0.0 copy-done.1
  225.1 5.2 %convolution_subtract_fusion = f32[2048,128]{1,0:T(8,128)S(1)} fusion(f32[2048,128]{1,0:T(8,128)S(1)} %copy-done.1, f32[2048,512]{1,0:T(8,128)} %constant_dynamic-update-slice_fusion, f32[512,128]{1,0:T(8,128)S(1)} %fusion.4), kind=kOutput, calls=%fused_computation | convolution fusion | flops 1610874880 | bytes 6553600 | tf_op jit(solution)/shard_map/dot_general | solution.py:481
  230.3 0.1 fusion.2
  230.4 0.0 copy-start.2
  230.4 1.0 copy-done.2
  (1 shorter events, 0.0 us)
Async XLA Ops:
  220.4 2.0 copy-start
  222.4 2.7 %copy-start.1 = (f32[2048,128]{1,0:T(8,128)S(1)}, f32[2048,128]{1,0:T(8,128)}, u32[]{:S(2)}) copy-start(f32[2048,128]{1,0:T(8,128)} %phe_hbm.1) | copy-start | bytes 3145732
  230.4 1.0 copy-start.2

commit v2 on v1

--- a/solution.py
+++ b/solution.py
@@ -12,6 +12,7 @@
 PIECES = 16
 GROUPS = 4
 HOP = 2
+PACE = 3
 DIAG_PIECES = 4
 MROWS = 256
 SLAB = 64
@@ -126,7 +127,7 @@
     def piece(buf, which, side, k, size):
         return buf.at[pl.ds(pl.multiple_of(which * BLK + (2 * k + side) * size, size), size)]
 
-    def ring_step(buf, size, sems, k_a, k_b, last, index_a, index_b):
+    def ring_step(buf, size, sems, k_a, k_b, last, index_a, index_b, paced=False):
         (asn, arc, bsn, brc, sas, sar, sbs, sbr) = sems
 
         @pl.when((k_a >= 0) & (k_a < last))
@@ -139,6 +140,12 @@
             def _():
                 d.wait_recv()
 
+            if paced:
+                @pl.when((pos == 0) & (k_a >= PACE))
+                def _():
+                    j = jnp.maximum(k_a - PACE, 0)
+                    remote(piece(buf, core, 0, j, size), asn.at[j], arc.at[j], tile=right).wait_send()
+
             @pl.when(pos < chips - 1)
             def _():
                 d.start()
@@ -154,6 +161,12 @@
             @pl.when(pos > 0)
             def _():
                 d.wait_recv()
+
+            if paced:
+                @pl.when((pos == 0) & (k_b >= PACE))
+                def _():
+                    j = jnp.maximum(k_b - PACE, 0)
+                    remote(piece(buf, core, 1, j, size), bsn.at[j], brc.at[j], tile=left).wait_send()
 
             @pl.when(pos != 1)
             def _():
@@ -166,15 +179,15 @@
         remote(piece(buf, 1 - core, 0, k, size), sas.at[i], sar.at[i], tile=sib).wait_recv()
         remote(piece(buf, 1 - core, 1, k, size), sbs.at[i], sbr.at[i], tile=sib).wait_recv()
 
-    def drain(buf, size, sems, k, i):
+    def drain(buf, size, sems, k, i, waiting=True):
         (asn, arc, bsn, brc, sas, sar, sbs, sbr) = sems
         ref_a, ref_b = piece(buf, core, 0, k, size), piece(buf, core, 1, k, size)
 
-        @pl.when(pos < chips - 1)
+        @pl.when((pos < chips - 1) & waiting)
         def _():
             remote(ref_a, asn.at[i], arc.at[i], tile=right).wait_send()
 
-        @pl.when(pos != 1)
+        @pl.when((pos != 1) & waiting)
         def _():
             remote(ref_b, bsn.at[i], brc.at[i], tile=left).wait_send()
 
@@ -197,7 +210,7 @@
         r = jnp.minimum(s, n_load - 1)
         part = jnp.sum(dos[pl.ds(pl.multiple_of(r * MROWS, MROWS), MROWS)].reshape(MROWS // 8, 8, snps), axis=0)
         total = total + jnp.where(s < n_load, part, 0.0)
-        ring_step(panels, psize, ring, s - pos, s - start_b, PIECES, s - pos, s - start_b)
+        ring_step(panels, psize, ring, s - pos, s - start_b, PIECES, s - pos, s - start_b, paced=True)
         return total
 
     first = max(n_load, PIECES // GROUPS + chips)
@@ -207,7 +220,7 @@
         count_copy(d).start()
 
     def ring_rest(s, carry):
-        ring_step(panels, psize, ring, s - pos, s - start_b, PIECES, s - pos, s - start_b)
+        ring_step(panels, psize, ring, s - pos, s - start_b, PIECES, s - pos, s - start_b, paced=True)
         return carry
 
     lax.fori_loop(n_load, first, ring_rest, 0)
@@ -278,7 +291,7 @@
     def slot(s, carry):
         for i in range(2):
             k_r = first + 2 * s + i
-            ring_step(panels, psize, ring, k_r - pos, k_r - start_b, PIECES, k_r - pos, k_r - start_b)
+            ring_step(panels, psize, ring, k_r - pos, k_r - start_b, PIECES, k_r - pos, k_r - start_b, paced=True)
 
         @pl.when(s == per - 1)
         def _():
@@ -401,7 +414,7 @@
     lax.fori_loop(0, n_chunk, finish, 0)
 
     def drain_ring(k, carry):
-        drain(panels, psize, ring, k, k)
+        drain(panels, psize, ring, k, k, (pos > 0) | (k >= PIECES - PACE))
         return carry
 
     lax.fori_loop(0, PIECES, drain_ring, 0)
@@ -468,17 +481,17 @@
     n_snp = lax.axis_size("snp")
     tile_index = lax.axis_index("tile")
     cross, inverse, upper, heads = gather_cross(dosages, phenotypes, n_tile, n_snp)
-    exact = functools.partial(lax.dot_general, precision=lax.Precision.HIGHEST, preferred_element_type=jnp.float32)
+    near = functools.partial(lax.dot_general, precision=lax.Precision.HIGH, preferred_element_type=jnp.float32)
     wide = 2 * BLK
     ordered = inverse.reshape(wide, 2, GROUPS, BLK // GROUPS).transpose(0, 2, 1, 3).reshape(wide, wide)
-    factor = exact(cross, ordered, NT)
+    factor = near(cross, ordered, NT)
     lower = upper.T
     solved = jnp.dot(inverse, heads, precision=lax.Precision.HIGHEST)
     head_rows = jnp.where(
         tile_index == 0, lower[:BLK], jnp.where(tile_index == 1, lower[BLK:], factor[:BLK])
     )
     factor = factor.at[:BLK].set(head_rows)
-    current = phenotypes - jnp.dot(factor, solved, precision=lax.Precision.HIGHEST)
+    current = phenotypes - jnp.dot(factor, solved, precision=lax.Precision.HIGH)
     head = jnp.where(tile_index == 0, solved[:BLK], jnp.where(tile_index == 1, solved[BLK:], current[:BLK]))
     return (factor, current.at[:BLK].set(head))
 

time: 232 us -> 228 us (0.983)
  matrix products: 16 us -> 11.6 us
    dot_general x2, matrix products: 13.7 us -> 9.4 us  [the longest x1 5.37 us: body(): factor = near(cross, ordered, NT)]
where the time goes in v2:
time: 228 us; the launch traced here: 227 us
  Pallas kernels  208 us (91%)
  matrix products  11.6 us (5%)
  local copies, waits for them, and re-layouts  5.9 us (3%)
    pallas_call x1, Pallas kernels, gather_cross(): pl.pallas_call(functools.partial(kernel, n_tile, n_snp), out_shape=(jax.S...  208 us
    dot_general x1, matrix products, body(): factor = near(cross, ordered, NT)  5.37 us

profile of v2, /device:TPU:2, one launch (start us, length us, event | category | flops | bytes accessed | tf_op | source)
XLA Modules:
  0.0 227.3 jit_solution(11182412300991560030)
XLA Ops:
  0.6 207.6 %shard_map.41 = (f32[2048,512]{1,0:T(8,128)}, f32[512,512]{1,0:T(8,128)}, f32[512,512]{1,0:T(8,128)}, f32[512,128]{1,0:T(8,128)}) custom-call(f32[2048,2048]{1,0:T(8,128)} %dos_hbm.1, f32[2048,128]{1,0:T(8,128)} %phe_hbm.1), custom_call_target="tpu_custom_call" | custom-call | tf_op jit(solution)/shard_map/pallas_call | solution.py:438
  208.3 2.2 fusion.4
  210.5 1.6 copy.6
  212.1 0.1 copy.7
  212.2 5.4 %fusion.3 = f32[2048,512]{1,0:T(8,128)S(1)} fusion(f32[2048,512]{1,0:T(8,128)} %get-tuple-element.30, f32[512,512]{0,1:T(8,128)S(1)} %bitcast.11), kind=kOutput, calls=%fused_computation.7 | convolution fusion | flops 3221225472 | bytes 9437184 | tf_op jit(solution)/shard_map/dot_general | solution.py:487
  217.6 0.0 copy-start
  217.6 2.0 copy-done
  219.6 0.0 copy-start.1
  219.7 0.2 copy.10
  219.9 1.4 fusion
  221.2 0.2 copy.9
  221.4 0.8 constant_dynamic-update-slice_fusion
  222.3 0.0 copy-done.1
  222.3 4.0 %convolution_subtract_fusion = f32[2048,128]{1,0:T(8,128)S(1)} fusion(f32[2048,128]{1,0:T(8,128)S(1)} %copy-done.1, f32[2048,512]{1,0:T(8,128)} %constant_dynamic-update-slice_fusion, f32[512,128]{1,0:T(8,128)S(1)} %fusion.4), kind=kOutput, calls=%fused_computation | convolution fusion | flops 805568512 | bytes 6553600 | tf_op jit(solution)/shard_map/dot_general | solution.py:494
  226.3 0.1 fusion.2
  226.4 0.0 copy-start.2
  226.4 1.0 copy-done.2
  (1 shorter events, 0.0 us)
Async XLA Ops:
  217.6 2.0 copy-start
  219.6 2.7 %copy-start.1 = (f32[2048,128]{1,0:T(8,128)S(1)}, f32[2048,128]{1,0:T(8,128)}, u32[]{:S(2)}) copy-start(f32[2048,128]{1,0:T(8,128)} %phe_hbm.1) | copy-start | bytes 3145732
  226.4 1.0 copy-start.2
